TPU v7x, 256 devices: a whole 4x4x8 slice. The times are simulated.
256 devices in a mesh: blk: 32 (over z, y_hi, core), dp: 8 (over x, y_lo).
Axes of the slice: x: 4, y: 4 (y_hi: 2, y_lo: 2; y = y_hi * 2 + y_lo), z: 8, core: 2. Of those that a mesh axis runs over, the one named last changes fastest.
Arguments:
- tokens: bfloat16 [65536, 4096], P(('blk', 'dp')), may hold values from -6 to 6
- cotangent: bfloat16 [65536, 4096], P(('blk', 'dp')), may hold values from -6 to 6
- gain: float32 [4096], replicated, may hold values from 0.1 to 1.9
- gate_up: bfloat16 [4096, 12288], P(None, 'blk'), may hold values from -0.09375 to 0.09375
- down: bfloat16 [6144, 4096], P('blk'), may hold values from -0.078125 to 0.078125
Outputs:
- grad_gate_up: float32 [4096, 12288], P('dp', 'blk')
- grad_down: float32 [6144, 4096], P('blk', 'dp')
All inputs are finite; a program needn't handle non-finite values.
Results may differ from a plain program's by a relative error of at most 0.0059.
Values may be sent and summed in bfloat16 or wider, within the bound.
A program may use at most 64 MiB of HBM per device.

v0:
```python
import math

import jax
import jax.numpy as jnp
from jax import lax
from jax.sharding import PartitionSpec as P


def passed_along(value, axis, steps):
    count = lax.axis_size(axis)
    pairs = [(source, (source + steps) % count) for source in range(count)]
    return lax.ppermute(value, axis, pairs)


def normed(rows, gain):
    values = rows.astype(jnp.float32)
    inverse = lax.rsqrt(jnp.mean(values * values, axis=-1, keepdims=True) + 1e-06)
    return (values * inverse * gain).astype(jnp.bfloat16)


def local_grads(normal_rows, upstream, gate_up, down, factor):
    width = down.shape[0]
    projected = jnp.dot(normal_rows, gate_up, preferred_element_type=jnp.float32)
    gate = projected[:, :width]
    upward = projected[:, width:]
    sigmoid_gate = jax.nn.sigmoid(gate)
    hidden = (gate * sigmoid_gate * upward).astype(jnp.bfloat16)
    back = jnp.einsum("td,fd->tf", upstream, down, preferred_element_type=jnp.float32)
    slope = sigmoid_gate * (1.0 + gate * (1.0 - sigmoid_gate))
    back_gate_up = jnp.concatenate(
        [back * upward * slope, back * gate * sigmoid_gate], axis=1
    ).astype(jnp.bfloat16)
    grad_gate_up = (
        jnp.einsum("td,tf->df", normal_rows, back_gate_up, preferred_element_type=jnp.float32)
        * factor
    )
    grad_down = (
        jnp.einsum("tf,td->fd", hidden, upstream, preferred_element_type=jnp.float32) * factor
    )
    return (grad_gate_up, grad_down)


def local(tokens, cotangent, gain, gate_up, down):
    factor = 1.0 / math.sqrt(3 * tokens.shape[0] * lax.axis_size("dp"))
    terms = []
    normal_rows = normed(tokens, gain)
    weights = (gate_up, down)
    for section_index in range(3):
        if section_index > 0:
            weights = passed_along((weights[0], weights[1]), "blk", 1)
        terms.append(local_grads(normal_rows, cotangent, weights[0], weights[1], factor))
    running = terms[2]
    for section_index in (1, 0):
        moved = passed_along(
            (running[0].astype(jnp.bfloat16), running[1].astype(jnp.bfloat16)), "blk", -1
        )
        running = (
            moved[0].astype(jnp.float32) + terms[section_index][0],
            moved[1].astype(jnp.float32) + terms[section_index][1],
        )
    summed = (
        lax.psum_scatter(running[0], "dp", scatter_dimension=0, tiled=True),
        lax.psum_scatter(running[1], "dp", scatter_dimension=1, tiled=True),
    )
    return (summed[0], summed[1])


def solution(mesh):
    in_specs = (P(("blk", "dp"), None), P(("blk", "dp"), None), P(), P(None, "blk"), P("blk", None))
    out_specs = (P("dp", "blk"), P("blk", "dp"))
    return jax.shard_map(local, mesh=mesh, in_specs=in_specs, out_specs=out_specs, check_vma=False)
```

profile of v0, /device:TPU:24, one launch (start us, length us, event | category | flops | bytes accessed | tf_op | source)
XLA Modules:
  0.0 474.5 jit_solution(11130879823183374343)
XLA Ops:
  7.2 0.0 copy-start
  7.2 0.0 reduce-scatter.5.cloned.1.call-start
  7.2 0.1 collective-permute-start.2
  7.3 38.4 %collective-permute-done.2 = bf16[4096,384]{1,0:T(8,128)(2,1)S(1)} collective-permute-done((bf16[4096,384]{1,0:T(8,128)(2,1)}, bf16[4096,384]{1,0:T(8,128)(2,1)S(1)}, u32[]{:S(2)}, u32[]{:S(2)}) %collective-permute-start.2) | collective-permute-done | bytes 3145760 | tf_op jit(solution)/shard_map/ppermute | solution.py:12
  45.7 0.0 collective-permute-start.3
  45.7 3.6 collective-permute-start
  49.3 2.1 fusion.1
  51.4 32.5 %collective-permute-done.3 = bf16[4096,384]{1,0:T(8,128)(2,1)S(1)} collective-permute-done((bf16[4096,384]{1,0:T(8,128)(2,1)S(1)}, bf16[4096,384]{1,0:T(8,128)(2,1)S(1)}, u32[]{:S(2)}, u32[]{:S(2)}) %collective-permute-start.3) | collective-permute-done | bytes 3145760 | tf_op jit(solution)/shard_map/ppermute | solution.py:12
  83.9 3.1 fusion.30
  87.0 0.0 copy-done
  87.1 0.0 copy-start.1
  87.1 0.0 copy-start.3
  87.1 0.6 fusion
  87.7 0.1 collective-permute-start.6
  87.8 29.8 %collective-permute-done = bf16[192,4096]{1,0:T(8,128)(2,1)S(1)} collective-permute-done((bf16[192,4096]{1,0:T(8,128)(2,1)}, bf16[192,4096]{1,0:T(8,128)(2,1)S(1)}, u32[]{:S(2)}, u32[]{:S(2)}) %collective-permute-start) | collective-permute-done | bytes 1572896 | tf_op jit(solution)/shard_map/ppermute | solution.py:12
  117.6 0.0 collective-permute-start.1
  117.6 0.0 copy-done.1
  117.6 0.0 copy-done.3
  117.6 1.6 fusion.27
  119.2 0.0 copy-done.6
  119.2 18.4 %collective-permute-done.6 = bf16[192,4096]{1,0:T(8,128)(2,1)S(1)} collective-permute-done((bf16[192,4096]{1,0:T(8,128)(2,1)S(1)}, bf16[192,4096]{1,0:T(8,128)(2,1)S(1)}, u32[]{:S(2)}, u32[]{:S(2)}) %collective-permute-start.6) | collective-permute-done | bytes 1572896 | tf_op jit(solution)/shard_map/ppermute | solution.py:12
  137.6 0.7 add_convert_fusion.1
  138.4 3.5 collective-permute-start.7
  141.8 47.7 %collective-permute-done.1 = bf16[192,4096]{1,0:T(8,128)(2,1)S(1)} collective-permute-done((bf16[192,4096]{1,0:T(8,128)(2,1)S(1)}, bf16[192,4096]{1,0:T(8,128)(2,1)S(1)}, u32[]{:S(2)}, u32[]{:S(2)}) %collective-permute-start.1) | collective-permute-done | bytes 1572896 | tf_op jit(solution)/shard_map/ppermute | solution.py:12
  189.5 0.9 multiply_convert_fusion.9
  190.4 0.0 copy-start.4
  190.4 3.1 multiply_convert_fusion
  193.5 0.0 collective-permute-start.4
  193.5 0.0 copy-done.4
  193.5 1.6 fusion.24
  195.1 0.6 convolution_multiply_fusion
  195.7 0.0 collective-permute-done.7
  195.7 2.1 convert_add_fusion
  197.8 0.0 reduce-scatter.5.cloned.1.call-update
  197.8 0.0 reduce-scatter.3.cloned.1.call-start
  197.9 0.0 copy-start.2
  197.9 2.4 multiply_convert_fusion.7
  200.3 87.3 %collective-permute-done.4 = bf16[4096,384]{1,0:T(8,128)(2,1)} collective-permute-done((bf16[4096,384]{1,0:T(8,128)(2,1)}, bf16[4096,384]{1,0:T(8,128)(2,1)}, u32[]{:S(2)}, u32[]{:S(2)}) %collective-permute-start.4) | collective-permute-done | bytes 3145760 | tf_op jit(solution)/shard_map/ppermute | solution.py:12
  287.6 0.0 copy-done.2
  287.6 3.5 add_convert_fusion
  291.1 3.5 collective-permute-start.5
  294.6 0.9 multiply_convert_fusion.5
  295.5 1.4 fusion.10
  297.0 32.5 %collective-permute-done.5 = bf16[4096,384]{1,0:T(8,128)(2,1)S(1)} collective-permute-done((bf16[4096,384]{1,0:T(8,128)(2,1)S(1)}, bf16[4096,384]{1,0:T(8,128)(2,1)S(1)}, u32[]{:S(2)}, u32[]{:S(2)}) %collective-permute-start.5) | collective-permute-done | bytes 3145760 | tf_op jit(solution)/shard_map/ppermute | solution.py:12
  329.4 3.4 multiply_add_fusion
  332.8 0.0 reduce-scatter.3.cloned.1.call-update
  332.8 0.0 reduce-scatter.5.cloned.1.call-done
  332.8 134.8 %reduce-scatter.3.cloned.1.call-done = f32[512,384]{1,0:T(8,128)} async-done(((f32[4096,384]{1,0:T(8,128)}), f32[512,384]{1,0:T(8,128)}) %reduce-scatter.3.cloned.1.call-update) | async-done | bytes 786448 | tf_op jit(solution)/shard_map/reduce_scatter | solution.py:62
  (4 shorter events, 0.0 us)
Async XLA Ops:
  7.2 79.9 %copy-start = (bf16[256,4096]{1,0:T(8,128)(2,1)S(1)}, bf16[256,4096]{1,0:T(8,128)(2,1)}, u32[]{:S(2)}) copy-start(bf16[256,4096]{1,0:T(8,128)(2,1)} %param.6) | copy-start | bytes 6291460
  7.2 325.7 %reduce-scatter.5.cloned.1.call-start = ((), (), s32[]{:S(2)}) async-start(), calls=%async_computation.3 | async-start | bytes 3538944 | tf_op jit(solution)/shard_map/reduce_scatter | solution.py:63
  7.2 38.5 %collective-permute-start.2 = (bf16[4096,384]{1,0:T(8,128)(2,1)}, bf16[4096,384]{1,0:T(8,128)(2,1)S(1)}, u32[]{:S(2)}, u32[]{:S(2)}) collective-permute-start(bf16[4096,384]{1,0:T(8,128)(2,1)} %param.8), channel_id=1, source_target_pairs={{0,8},{8,16},{16,24},{24,32},{32,40},{40,48},{48,56},{56,64},{64,7... | collective-permute-start | bytes 9437192 | tf_op jit(solution)/shard_map/ppermute | solution.py:12
  45.7 38.2 %collective-permute-start.3 = (bf16[4096,384]{1,0:T(8,128)(2,1)S(1)}, bf16[4096,384]{1,0:T(8,128)(2,1)S(1)}, u32[]{:S(2)}, u32[]{:S(2)}) collective-permute-start(bf16[4096,384]{1,0:T(8,128)(2,1)S(1)} %collective-permute-done.2), channel_id=1, source_target_pairs={{0,8},{8,16},{16,24},{24,32},{32,40},{40,48},{48,56},{56,64},{64,7... | collective-permute-start | bytes 9437192 | tf_op jit(solution)/shard_map/ppermute | solution.py:12
  45.7 71.9 %collective-permute-start = (bf16[192,4096]{1,0:T(8,128)(2,1)}, bf16[192,4096]{1,0:T(8,128)(2,1)S(1)}, u32[]{:S(2)}, u32[]{:S(2)}) collective-permute-start(bf16[192,4096]{1,0:T(8,128)(2,1)} %param.9), channel_id=1, source_target_pairs={{0,8},{8,16},{16,24},{24,32},{32,40},{40,48},{48,56},{56,64},{64,7... | collective-permute-start | bytes 4718600 | tf_op jit(solution)/shard_map/ppermute | solution.py:12
  87.1 30.6 %copy-start.1 = (bf16[256,4096]{1,0:T(8,128)(2,1)S(1)}, bf16[256,4096]{1,0:T(8,128)(2,1)}, u32[]{:S(2)}) copy-start(bf16[256,4096]{1,0:T(8,128)(2,1)} %param.5) | copy-start | bytes 6291460
  87.1 30.6 %copy-start.3 = (f32[4096]{0:T(1024)S(1)}, f32[4096]{0:T(1024)}, u32[]{:S(2)}) copy-start(f32[4096]{0:T(1024)} %param.7) | copy-start | bytes 49156
  87.7 49.9 %collective-permute-start.6 = (bf16[192,4096]{1,0:T(8,128)(2,1)S(1)}, bf16[192,4096]{1,0:T(8,128)(2,1)S(1)}, u32[]{:S(2)}, u32[]{:S(2)}) collective-permute-start(bf16[192,4096]{1,0:T(8,128)(2,1)S(1)} %fusion), channel_id=1, source_target_pairs={{0,248},{8,0},{16,8},{24,16},{32,24},{40,32},{48,40},{56,48},{64,5... | collective-permute-start | bytes 4718600 | tf_op jit(solution)/shard_map/ppermute | solution.py:12
  117.6 1.6 copy-start.6
  117.6 71.9 %collective-permute-start.1 = (bf16[192,4096]{1,0:T(8,128)(2,1)S(1)}, bf16[192,4096]{1,0:T(8,128)(2,1)S(1)}, u32[]{:S(2)}, u32[]{:S(2)}) collective-permute-start(bf16[192,4096]{1,0:T(8,128)(2,1)S(1)} %collective-permute-done), channel_id=1, source_target_pairs={{0,8},{8,16},{16,24},{24,32},{32,40},{40,48},{48,56},{56,64},{64,7... | collective-permute-start | bytes 4718600 | tf_op jit(solution)/shard_map/ppermute | solution.py:12
  138.4 57.3 %collective-permute-start.7 = (bf16[192,4096]{1,0:T(8,128)(2,1)S(1)}, bf16[192,4096]{1,0:T(8,128)(2,1)S(1)}, u32[]{:S(2)}, u32[]{:S(2)}) collective-permute-start(bf16[192,4096]{1,0:T(8,128)(2,1)S(1)} %add_convert_fusion.1), channel_id=1, source_target_pairs={{0,248},{8,0},{16,8},{24,16},{32,24},{40,32},{48,40},{56,48},{64,5... | collective-permute-start | bytes 4718600 | tf_op jit(solution)/shard_map/ppermute | solution.py:12
  190.4 3.1 copy-start.4
  193.5 94.1 %collective-permute-start.4 = (bf16[4096,384]{1,0:T(8,128)(2,1)}, bf16[4096,384]{1,0:T(8,128)(2,1)}, u32[]{:S(2)}, u32[]{:S(2)}) collective-permute-start(bf16[4096,384]{1,0:T(8,128)(2,1)} %multiply_convert_fusion), channel_id=1, source_target_pairs={{0,248},{8,0},{16,8},{24,16},{32,24},{40,32},{48,40},{56,48},{64,5... | collective-permute-start | bytes 9437192 | tf_op jit(solution)/shard_map/ppermute | solution.py:12
  197.8 269.8 %reduce-scatter.3.cloned.1.call-start = ((), (), s32[]{:S(2)}) async-start(), calls=%async_computation.2 | async-start | bytes 7077888 | tf_op jit(solution)/shard_map/reduce_scatter | solution.py:62
  197.9 89.7 %copy-start.2 = (bf16[256,4096]{1,0:T(8,128)(2,1)S(1)}, bf16[256,4096]{1,0:T(8,128)(2,1)}, u32[]{:S(2)}) copy-start(bf16[256,4096]{1,0:T(8,128)(2,1)} %param.5) | copy-start | bytes 6291460
  287.6 7.0 %copy-start.5 = (bf16[192,4096]{1,0:T(8,128)(2,1)S(1)}, bf16[192,4096]{1,0:T(8,128)(2,1)}, u32[]{:S(2)}) copy-start(bf16[192,4096]{1,0:T(8,128)(2,1)} %param.9) | copy-start | bytes 4718596
  291.1 38.3 %collective-permute-start.5 = (bf16[4096,384]{1,0:T(8,128)(2,1)S(1)}, bf16[4096,384]{1,0:T(8,128)(2,1)S(1)}, u32[]{:S(2)}, u32[]{:S(2)}) collective-permute-start(bf16[4096,384]{1,0:T(8,128)(2,1)S(1)} %add_convert_fusion), channel_id=1, source_target_pairs={{0,248},{8,0},{16,8},{24,16},{32,24},{40,32},{48,40},{56,48},{64,5... | collective-permute-start | bytes 9437192 | tf_op jit(solution)/shard_map/ppermute | solution.py:12
Sparse Core Ops, SparseCore 0:
  197.9 89.7 reduce-scatter.4
  332.9 134.6 reduce-scatter.2
where the time goes:
time: 476 us; the launch traced here: 474 us
  waiting for transfers between devices  421 us (88%)
  matrix products  20.4 us (4%)
  between operations  14.2 us (3%)
  starting transfers between devices  10.8 us (2%)
  other arithmetic  7.56 us (2%)
    ppermute x8, waiting for transfers between devices, passed_along(): return lax.ppermute(value, axis, pairs)  287 us
    reduce_scatter x1, waiting for transfers between devices, local(): lax.psum_scatter(running[0], 'dp', scatter_dimension=0, tiled=True)  135 us
    ppermute x8, starting transfers between devices, passed_along(): return lax.ppermute(value, axis, pairs)  10.8 us
  transfers between devices with their start and end apart: 10, of which 8 were waited for; matrix products, arithmetic and copies ran while one was open for 6% of the time, Pallas kernels for 0%

commit v1 on v0

v1 whole, which is shorter than its diff:
```python
import functools
import math

import jax
import jax.numpy as jnp
from jax import lax
from jax.experimental import pallas as pl
from jax.experimental.pallas import tpu as pltpu
from jax.sharding import PartitionSpec as P

MESH = pl.DeviceIdType.MESH
F32 = jnp.float32
BF16 = jnp.bfloat16

TOK = 256
D = 4096
FB = 192
SL = D // 8
CH = 64
NCH = TOK // CH

ORDERS = (("a", "b", "y"), ("b", "y", "a"), ("y", "a", "b"))


def flip(v):
    return v + 1 - 2 * lax.rem(v, 2)


def moved(d, toggle):
    x, y = d // 2, lax.rem(d, 2)
    x = x + toggle["a"] * (1 - 2 * lax.rem(x, 2))
    x = lax.rem(x + toggle["b"] * (2 * lax.rem(x, 2) - 1) + 4, 4)
    y = y + toggle["y"] * (1 - 2 * y)
    return 2 * x + y


def partner(d, dim):
    return moved(d, {name: int(name == dim) for name in "aby"})


def share_rs(d, p, r):
    o = ORDERS[p]
    return moved(d, {o[0]: r // 4, o[1]: lax.rem(r // 2, 2), o[2]: lax.rem(r, 2)})


def share_ag(d, p, r):
    o = ORDERS[p]
    return moved(d, {o[2]: r // 4, o[1]: lax.rem(r // 2, 2), o[0]: lax.rem(r, 2)})


def columns(j, width):
    return pl.ds(pl.multiple_of(j * width, width), width)


def kernel(
    scale,
    tok, cot, gain, gu, dn,
    o_gu, o_dn,
    nrm, ctg, wg, wd, wf, wfd, proj, act, actf, snd, rcv, rcvf, acc, back, ret,
    ld_sem, ws_s, ws_r, ag_s, ag_r, rs_s, rs_r, rf_s, rf_r,
    tk_s, tk_r, fw_s, fw_r, t1_s, t1_r, rt_s, rt_r,
):
    b = lax.axis_index("blk")
    d = lax.axis_index("dp")
    core = lax.rem(b, 2)
    n_blk = 32
    nxt = lax.rem(b + 2, n_blk)
    prv = lax.rem(b + n_blk - 2, n_blk)
    other = flip(b)
    df = flip(d)
    own = pl.ds(pl.multiple_of(core * TOK, TOK), TOK)

    def load(i, src, dst):
        return pltpu.make_async_copy(src, dst, ld_sem.at[i])

    def remote(src, dst, ss, rs, tb, td):
        return pltpu.make_async_remote_copy(
            src_ref=src, dst_ref=dst, send_sem=ss, recv_sem=rs,
            device_id=(tb, td), device_id_type=MESH,
        )

    ld_tok = load(0, tok, nrm.at[own])
    ld_cot = load(1, cot, ctg.at[own])
    ld_wg = load(2, gu, wg)
    ld_wd = load(3, dn, wd)
    ld_tok.start()
    ld_cot.start()
    ld_wg.start()
    ld_wd.start()

    barrier = pltpu.get_barrier_semaphore()
    greeted = [(other, d), (nxt, df), (prv, df)] + [(b, partner(d, k)) for k in "aby"]
    for tb, td in greeted:
        pl.semaphore_signal(barrier, inc=1, device_id=(tb, td), device_id_type=MESH)
    pl.semaphore_wait(barrier, len(greeted))

    def weight_slice(p):
        if p == 2:
            return remote(dn.at[:, columns(df, SL)], wfd.at[0], ws_s.at[2], ws_r.at[2], nxt, df)
        rows = pl.ds(pl.multiple_of(df * SL + p * 256, 256), 256)
        return remote(gu.at[rows, :], wf.at[p, 0], ws_s.at[p], ws_r.at[p], nxt, df)

    def gather(p, step):
        n = 2 ** step
        ref = wfd if p == 2 else wf.at[p]
        return remote(
            ref.at[pl.ds(0, n)], ref.at[pl.ds(n, n)],
            ag_s.at[p, step], ag_r.at[p, step], b, partner(d, ORDERS[p][step]),
        )

    def token_piece(i, kind):
        here = pl.ds(pl.multiple_of(i * CH, CH), CH)
        there = pl.ds(pl.multiple_of(2 * TOK + i * CH, CH), CH)
        if kind == 0:
            return remote(cot.at[here], ctg.at[there], tk_s.at[i, 0], tk_r.at[i, 0], prv, df)
        return remote(nrm.at[here], nrm.at[there], tk_s.at[i, 1], tk_r.at[i, 1], prv, df)

    def forwarded(i, kind):
        there = pl.ds(pl.multiple_of(2 * TOK + i * CH, CH), CH)
        ref = nrm if kind else ctg
        return remote(ref.at[there], ref.at[there], fw_s.at[i, kind], fw_r.at[i, kind], other, d)

    mid = pl.ds(TOK, TOK)
    mid_cot = remote(cot, ctg.at[mid], t1_s.at[0], t1_r.at[0], other, d)
    mid_nrm = remote(nrm.at[mid], nrm.at[mid], t1_s.at[1], t1_r.at[1], other, d)

    def returned(p):
        return remote(back.at[p], ret.at[p], rt_s.at[p], rt_r.at[p], prv, df)

    def normalise(row0, n):
        def body(i, _):
            rows = pl.ds(pl.multiple_of(row0 + i * 16, 16), 16)
            v = nrm[rows, :].astype(F32)
            inv = lax.rsqrt(jnp.mean(v * v, axis=-1, keepdims=True) + 1e-06)
            nrm[rows, :] = (v * inv * gain[...]).astype(BF16)
            return 0

        lax.fori_loop(0, n // 16, body, 0)

    def forward(row0, n, to):
        rows = pl.ds(pl.multiple_of(row0, CH), n)
        out = pl.ds(pl.multiple_of(to, CH), n)
        proj[out, 0:384] = jnp.dot(nrm[rows, :], wg[...], preferred_element_type=F32)
        proj[out, 384:576] = lax.dot_general(
            ctg[rows, :], wd[...], (((1,), (1,)), ((), ())), preferred_element_type=F32
        )

    def activate(dst, cols):
        t = proj[...].T
        gate, up, bk = t[0:FB], t[FB:2 * FB], t[2 * FB:3 * FB]
        s = jax.nn.sigmoid(gate)
        dst[0:FB, cols] = (bk * up * (s * (1.0 + gate * (1.0 - s)))).astype(BF16)
        dst[FB:2 * FB, cols] = (bk * gate * s).astype(BF16)
        dst[2 * FB:3 * FB, cols] = (gate * s * up).astype(BF16)

    def reduce_scatter(term, r_ref, s_sem, r_sem):
        def copy(p, slot, step):
            return remote(
                snd.at[p, slot], r_ref.at[p, slot], s_sem.at[p, slot], r_sem.at[p, slot],
                b, partner(d, ORDERS[p][step]),
            )

        def first(i, _):
            q = 3 - 2 * lax.rem(i, 2) - i // 2

            def put(p, v):
                snd[p, q] = v.astype(BF16)

            term(q + 4, put)
            for p in range(3):
                copy(p, q, 0).start()
            return 0

        def kept(i, _):
            q = 3 - 2 * lax.rem(i, 2) - i // 2

            def put(p, v):
                acc[p, q] = v

            term(q, put)
            return 0

        lax.fori_loop(0, 4, first, 0)
        lax.fori_loop(0, 4, kept, 0)
        for q in (3, 1, 2, 0):
            for p in range(3):
                copy(p, q, 0).wait_recv()
                v = acc[p, q] + r_ref[p, q].astype(F32)
                if q >= 2:
                    snd[p, q + 2] = v.astype(BF16)
                    copy(p, q + 2, 1).start()
                else:
                    acc[p, q] = v
        for p in range(3):
            copy(p, 5, 1).wait_recv()
            snd[p, 6] = (acc[p, 1] + r_ref[p, 5].astype(F32)).astype(BF16)
            copy(p, 6, 2).start()
        for p in range(3):
            copy(p, 4, 1).wait_recv()
            acc[p, 0] = acc[p, 0] + r_ref[p, 4].astype(F32)
        for p in range(3):
            copy(p, 6, 2).wait_recv()
            acc[p, 0] = acc[p, 0] + r_ref[p, 6].astype(F32)
        for p in range(3):
            for slot, step in [(k, 0) for k in range(4)] + [(4, 1), (5, 1), (6, 2)]:
                copy(p, slot, step).wait_send()

    def grads(a_ref, a_cols, tok_rows, share, put):
        for p in range(3):
            x = ctg if p == 2 else nrm
            put(p, jnp.dot(
                a_ref[p * FB:(p + 1) * FB, a_cols],
                x[tok_rows, columns(share(p), SL)],
                preferred_element_type=F32,
            ))

    @pl.when(core == 0)
    def _():
        ld_tok.wait()
        for i in range(2):
            token_piece(i, 0).start()
            normalise(i * CH, CH)
            token_piece(i, 1).start()
        normalise(2 * CH, TOK - 2 * CH)
        ld_cot.wait()
        ld_wg.wait()
        ld_wd.wait()
        forward(0, TOK, 0)
        activate(act, pl.ds(0, TOK))
        mid_cot.wait_recv()
        mid_nrm.wait_recv()
        forward(TOK, TOK, 0)
        activate(act, pl.ds(TOK, TOK))

        def piece(i, _):
            for kind in (0, 1):
                token_piece(i, kind).wait_recv()
                forwarded(i, kind).start()

            @pl.when(i + 2 < NCH)
            def _():
                for kind in (0, 1):
                    token_piece(i + 2, kind).start()

            forward(2 * TOK + i * CH, CH, i * CH)
            return 0

        lax.fori_loop(0, NCH, piece, 0)
        activate(act, pl.ds(2 * TOK, TOK))

    @pl.when(core == 1)
    def _():
        for p in range(3):
            weight_slice(p).start()
        mid_cot.start()
        ld_tok.wait()
        normalise(TOK, TOK)
        mid_nrm.start()
        for p in range(3):
            weight_slice(p).wait_recv()
            gather(p, 0).start()
        for p in range(3):
            gather(p, 0).wait_recv()
            gather(p, 1).start()
        ld_cot.wait()
        ld_wg.wait()
        ld_wd.wait()
        for p in range(3):
            gather(p, 1).wait_recv()
            gather(p, 2).start()
        forward(TOK, TOK, 0)
        activate(act, pl.ds(TOK, TOK))

        proj[...] = jnp.zeros_like(proj)

        def partial(r, _):
            for p in range(2):
                j = share_ag(d, p, r)
                cols = pl.ds(pl.multiple_of(j * SL + p * 256, 256), 256)
                proj[:, 0:384] += jnp.dot(nrm[mid, cols], wf[p, r], preferred_element_type=F32)
            proj[:, 384:576] += lax.dot_general(
                ctg[mid, columns(share_ag(d, 2, r), SL)], wfd[r],
                (((1,), (1,)), ((), ())), preferred_element_type=F32,
            )
            return 0

        lax.fori_loop(0, 4, partial, 0)
        for p in range(3):
            gather(p, 2).wait_recv()
        lax.fori_loop(4, 8, partial, 0)
        activate(actf, pl.ds(0, TOK))

        def term(r, put):
            grads(actf, slice(0, TOK), mid, lambda p: flip(share_rs(d, p, r)), put)

        reduce_scatter(term, rcvf, rf_s, rf_r)
        for p in range(3):
            back[p] = acc[p, 0].astype(BF16)
            returned(p).start()

        def piece(i, _):
            for kind in (0, 1):
                forwarded(i, kind).wait_recv()
            forward(2 * TOK + i * CH, CH, i * CH)
            return 0

        lax.fori_loop(0, NCH, piece, 0)
        activate(act, pl.ds(2 * TOK, TOK))

    def own_term(r, put):
        @pl.when(core == 0)
        def _():
            grads(act, slice(0, 3 * TOK), pl.ds(0, 3 * TOK), lambda p: share_rs(d, p, r), put)

        @pl.when(core == 1)
        def _():
            grads(act, slice(TOK, 3 * TOK), pl.ds(TOK, 2 * TOK), lambda p: share_rs(d, p, r), put)

    reduce_scatter(own_term, rcv, rs_s, rs_r)

    @pl.when(core == 1)
    def _():
        for p in range(3):
            returned(p).wait_recv()
            acc[p, 0] = acc[p, 0] + ret[p].astype(F32)

    o_gu[:, 0:FB] = (acc[0, 0] * scale).T
    o_gu[:, FB:2 * FB] = (acc[1, 0] * scale).T
    o_dn[...] = acc[2, 0] * scale

    @pl.when(core == 0)
    def _():
        for i in range(NCH):
            for kind in (0, 1):
                token_piece(i, kind).wait_send()
                forwarded(i, kind).wait_send()

    @pl.when(core == 1)
    def _():
        mid_cot.wait_send()
        mid_nrm.wait_send()
        for p in range(3):
            weight_slice(p).wait_send()
            returned(p).wait_send()
            for step in range(3):
                gather(p, step).wait_send()


def local(tokens, cotangent, gain, gate_up, down):
    scale = 1.0 / math.sqrt(3 * TOK * 8)
    anywhere = pl.BlockSpec(memory_space=pl.ANY)
    vmem = pl.BlockSpec(memory_space=pltpu.VMEM)
    dma = pltpu.SemaphoreType.DMA
    return pl.pallas_call(
        functools.partial(kernel, scale),
        out_shape=(
            jax.ShapeDtypeStruct((SL, 2 * FB), F32),
            jax.ShapeDtypeStruct((FB, SL), F32),
        ),
        in_specs=[anywhere, anywhere, vmem, anywhere, anywhere],
        out_specs=(vmem, vmem),
        scratch_shapes=[
            pltpu.VMEM((3 * TOK, D), BF16),
            pltpu.VMEM((3 * TOK, D), BF16),
            pltpu.VMEM((D, 2 * FB), BF16),
            pltpu.VMEM((FB, D), BF16),
            pltpu.VMEM((2, 8, 256, 2 * FB), BF16),
            pltpu.VMEM((8, FB, SL), BF16),
            pltpu.VMEM((TOK, 3 * FB), F32),
            pltpu.VMEM((3 * FB, 3 * TOK), BF16),
            pltpu.VMEM((3 * FB, TOK), BF16),
            pltpu.VMEM((3, 7, FB, SL), BF16),
            pltpu.VMEM((3, 7, FB, SL), BF16),
            pltpu.VMEM((3, 7, FB, SL), BF16),
            pltpu.VMEM((3, 4, FB, SL), F32),
            pltpu.VMEM((3, FB, SL), BF16),
            pltpu.VMEM((3, FB, SL), BF16),
            dma((4,)),
            dma((3,)), dma((3,)), dma((3, 3)), dma((3, 3)),
            dma((3, 7)), dma((3, 7)), dma((3, 7)), dma((3, 7)),
            dma((NCH, 2)), dma((NCH, 2)), dma((NCH, 2)), dma((NCH, 2)),
            dma((2,)), dma((2,)), dma((3,)), dma((3,)),
        ],
        compiler_params=pltpu.CompilerParams(
            collective_id=0, has_side_effects=True, vmem_limit_bytes=58 << 20
        ),
        name="grads",
    )(tokens, cotangent, gain.reshape(1, D), gate_up, down)


def solution(mesh):
    in_specs = (P(("blk", "dp"), None), P(("blk", "dp"), None), P(), P(None, "blk"), P("blk", None))
    out_specs = (P("dp", "blk"), P("blk", "dp"))
    return jax.shard_map(local, mesh=mesh, in_specs=in_specs, out_specs=out_specs, check_vma=False)
```

time: 476 us -> 140 us (0.29)
  the two profiles are of different devices: /device:TPU:24 before, /device:TPU:17 now
where the time goes in v1:
time: 140 us
  Pallas kernels  135 us (96%)
  local copies, waits for them, and re-layouts  3.83 us (3%)
    pallas_call x1, Pallas kernels, local(): pl.pallas_call(functools.partial(kernel, scale), out_shape=(jax.ShapeDtyp...  135 us
    unnamed x2, local copies, waits for them, and re-layouts  3.83 us

profile of v1, /device:TPU:17, one launch (start us, length us, event | category | flops | bytes accessed | tf_op | source)
XLA Modules:
  0.0 139.9 jit_solution(10228408012857945848)
XLA Ops:
  0.6 135.4 %grads.1 = (f32[512,384]{1,0:T(8,128)}, f32[192,512]{1,0:T(8,128)}) custom-call(bf16[256,4096]{1,0:T(8,128)(2,1)} %tok.1, bf16[256,4096]{1,0:T(8,128)(2,1)} %cot.1, f32[1,4096]{1,0:T(1,128)} %bitcast.1, bf16[4096,384]{1,0:T(8,128)(2,1)} %gu.1, bf16[192,4096]{1,0:T(8,128)(2,1)} %dn.1), custom_call_target="tpu_custom_call" | custom-call | tf_op jit(solution)/shard_map/grads/pallas_call | solution.py:354
  136.1 2.1 %copy.9 = f32[512,384]{1,0:T(8,128)} copy(f32[512,384]{1,0:T(8,128)} %get-tuple-element.4) | data formatting | bytes 1572864
  138.1 1.8 %copy.10 = f32[192,512]{1,0:T(8,128)} copy(f32[192,512]{1,0:T(8,128)} %get-tuple-element.5) | data formatting | bytes 786432

commit v2 on v1

--- a/solution.py
+++ b/solution.py
@@ -58,7 +58,7 @@
     o_gu, o_dn,
     nrm, ctg, wg, wd, wf, wfd, proj, act, actf, snd, rcv, rcvf, acc, back, ret,
     ld_sem, ws_s, ws_r, ag_s, ag_r, rs_s, rs_r, rf_s, rf_r,
-    tk_s, tk_r, fw_s, fw_r, t1_s, t1_r, rt_s, rt_r,
+    tk_s, tk_r, fw_s, fw_r, t1_s, t1_r, rt_s, rt_r, go,
 ):
     b = lax.axis_index("blk")
     d = lax.axis_index("dp")
@@ -67,6 +67,7 @@
     nxt = lax.rem(b + 2, n_blk)
     prv = lax.rem(b + n_blk - 2, n_blk)
     other = flip(b)
+    beside = lax.rem(b + n_blk - 1 + 2 * core, n_blk)
     df = flip(d)
     own = pl.ds(pl.multiple_of(core * TOK, TOK), TOK)
 
@@ -89,7 +90,7 @@
     ld_wd.start()
 
     barrier = pltpu.get_barrier_semaphore()
-    greeted = [(other, d), (nxt, df), (prv, df)] + [(b, partner(d, k)) for k in "aby"]
+    greeted = [(other, d), (nxt, df), (prv, df), (beside, df)] + [(b, partner(d, k)) for k in "aby"]
     for tb, td in greeted:
         pl.semaphore_signal(barrier, inc=1, device_id=(tb, td), device_id_type=MESH)
     pl.semaphore_wait(barrier, len(greeted))
@@ -217,11 +218,11 @@
     @pl.when(core == 0)
     def _():
         ld_tok.wait()
+        normalise(0, TOK)
+        pl.semaphore_wait(go, 1)
         for i in range(2):
             token_piece(i, 0).start()
-            normalise(i * CH, CH)
             token_piece(i, 1).start()
-        normalise(2 * CH, TOK - 2 * CH)
         ld_cot.wait()
         ld_wg.wait()
         ld_wd.wait()
@@ -259,6 +260,7 @@
         for p in range(3):
             weight_slice(p).wait_recv()
             gather(p, 0).start()
+        pl.semaphore_signal(go, inc=1, device_id=(beside, df), device_id_type=MESH)
         for p in range(3):
             gather(p, 0).wait_recv()
             gather(p, 1).start()
@@ -380,6 +382,7 @@
             dma((3, 7)), dma((3, 7)), dma((3, 7)), dma((3, 7)),
             dma((NCH, 2)), dma((NCH, 2)), dma((NCH, 2)), dma((NCH, 2)),
             dma((2,)), dma((2,)), dma((3,)), dma((3,)),
+            pltpu.SemaphoreType.REGULAR,
         ],
         compiler_params=pltpu.CompilerParams(
             collective_id=0, has_side_effects=True, vmem_limit_bytes=58 << 20

time: 140 us -> 117 us (0.84)
  the two profiles are of different devices: /device:TPU:17 before, /device:TPU:24 now
where the time goes in v2:
time: 117 us; the launch traced here: 115 us
  Pallas kernels  111 us (95%)
  local copies, waits for them, and re-layouts  3.83 us (3%)
    pallas_call x1, Pallas kernels, local(): pl.pallas_call(functools.partial(kernel, scale), out_shape=(jax.ShapeDtyp...  111 us
    unnamed x2, local copies, waits for them, and re-layouts  3.83 us

profile of v2, /device:TPU:24, one launch (start us, length us, event | category | flops | bytes accessed | tf_op | source)
XLA Modules:
  0.0 115.3 jit_solution(2500903542724128934)
XLA Ops:
  0.6 110.8 %grads.1 = (f32[512,384]{1,0:T(8,128)}, f32[192,512]{1,0:T(8,128)}) custom-call(bf16[256,4096]{1,0:T(8,128)(2,1)} %tok.1, bf16[256,4096]{1,0:T(8,128)(2,1)} %cot.1, f32[1,4096]{1,0:T(1,128)} %bitcast.1, bf16[4096,384]{1,0:T(8,128)(2,1)} %gu.1, bf16[192,4096]{1,0:T(8,128)(2,1)} %dn.1), custom_call_target="tpu_custom_call" | custom-call | tf_op jit(solution)/shard_map/grads/pallas_call | solution.py:356
  111.4 2.1 %copy.9 = f32[512,384]{1,0:T(8,128)} copy(f32[512,384]{1,0:T(8,128)} %get-tuple-element.4) | data formatting | bytes 1572864
  113.5 1.8 %copy.10 = f32[192,512]{1,0:T(8,128)} copy(f32[192,512]{1,0:T(8,128)} %get-tuple-element.5) | data formatting | bytes 786432

commit v3 on v2

--- a/solution.py
+++ b/solution.py
@@ -52,10 +52,15 @@
     return pl.ds(pl.multiple_of(j * width, width), width)
 
 
+def finish(scale, sums, o_gu, o_dn):
+    o_gu[:, 0:FB] = (sums[0] * scale).T
+    o_gu[:, FB:2 * FB] = (sums[1] * scale).T
+    o_dn[...] = sums[2] * scale
+
+
 def kernel(
-    scale,
     tok, cot, gain, gu, dn,
-    o_gu, o_dn,
+    out,
     nrm, ctg, wg, wd, wf, wfd, proj, act, actf, snd, rcv, rcvf, acc, back, ret,
     ld_sem, ws_s, ws_r, ag_s, ag_r, rs_s, rs_r, rf_s, rf_r,
     tk_s, tk_r, fw_s, fw_r, t1_s, t1_r, rt_s, rt_r, go,
@@ -85,9 +90,11 @@
     ld_wg = load(2, gu, wg)
     ld_wd = load(3, dn, wd)
     ld_tok.start()
-    ld_cot.start()
-    ld_wg.start()
-    ld_wd.start()
+
+    def load_rest():
+        ld_cot.start()
+        ld_wg.start()
+        ld_wd.start()
 
     barrier = pltpu.get_barrier_semaphore()
     greeted = [(other, d), (nxt, df), (prv, df), (beside, df)] + [(b, partner(d, k)) for k in "aby"]
@@ -101,13 +108,15 @@
         rows = pl.ds(pl.multiple_of(df * SL + p * 256, 256), 256)
         return remote(gu.at[rows, :], wf.at[p, 0], ws_s.at[p], ws_r.at[p], nxt, df)
 
-    def gather(p, step):
-        n = 2 ** step
+    def gather(p, src, step):
         ref = wfd if p == 2 else wf.at[p]
+        dst = src + 2 ** step
         return remote(
-            ref.at[pl.ds(0, n)], ref.at[pl.ds(n, n)],
-            ag_s.at[p, step], ag_r.at[p, step], b, partner(d, ORDERS[p][step]),
+            ref.at[src], ref.at[dst], ag_s.at[p, dst - 1], ag_r.at[p, dst - 1],
+            b, partner(d, ORDERS[p][step]),
         )
+
+    gathers = [(0, 0), (0, 1), (0, 2), (1, 1), (1, 2), (2, 2), (3, 2)]
 
     def token_piece(i, kind):
         here = pl.ds(pl.multiple_of(i * CH, CH), CH)
@@ -154,7 +163,7 @@
         dst[FB:2 * FB, cols] = (bk * gate * s).astype(BF16)
         dst[2 * FB:3 * FB, cols] = (gate * s * up).astype(BF16)
 
-    def reduce_scatter(term, r_ref, s_sem, r_sem):
+    def reduce_scatter(term, r_ref, s_sem, r_sem, beside_it=None):
         def copy(p, slot, step):
             return remote(
                 snd.at[p, slot], r_ref.at[p, slot], s_sem.at[p, slot], r_sem.at[p, slot],
@@ -183,6 +192,8 @@
 
         lax.fori_loop(0, 4, first, 0)
         lax.fori_loop(0, 4, kept, 0)
+        if beside_it is not None:
+            beside_it(0)
         for q in (3, 1, 2, 0):
             for p in range(3):
                 copy(p, q, 0).wait_recv()
@@ -192,6 +203,8 @@
                     copy(p, q + 2, 1).start()
                 else:
                     acc[p, q] = v
+        if beside_it is not None:
+            beside_it(1)
         for p in range(3):
             copy(p, 5, 1).wait_recv()
             snd[p, 6] = (acc[p, 1] + r_ref[p, 5].astype(F32)).astype(BF16)
@@ -217,10 +230,11 @@
 
     @pl.when(core == 0)
     def _():
+        load_rest()
         ld_tok.wait()
         normalise(0, TOK)
         pl.semaphore_wait(go, 1)
-        for i in range(2):
+        for i in range(NCH):
             token_piece(i, 0).start()
             token_piece(i, 1).start()
         ld_cot.wait()
@@ -238,11 +252,6 @@
                 token_piece(i, kind).wait_recv()
                 forwarded(i, kind).start()
 
-            @pl.when(i + 2 < NCH)
-            def _():
-                for kind in (0, 1):
-                    token_piece(i + 2, kind).start()
-
             forward(2 * TOK + i * CH, CH, i * CH)
             return 0
 
@@ -254,24 +263,31 @@
         for p in range(3):
             weight_slice(p).start()
         mid_cot.start()
+        load_rest()
         ld_tok.wait()
         normalise(TOK, TOK)
         mid_nrm.start()
         for p in range(3):
             weight_slice(p).wait_recv()
-            gather(p, 0).start()
-        pl.semaphore_signal(go, inc=1, device_id=(beside, df), device_id_type=MESH)
-        for p in range(3):
-            gather(p, 0).wait_recv()
-            gather(p, 1).start()
+            for step in range(3):
+                gather(p, 0, step).start()
+            if p == 1:
+                pl.semaphore_signal(go, inc=1, device_id=(beside, df), device_id_type=MESH)
         ld_cot.wait()
         ld_wg.wait()
         ld_wd.wait()
         for p in range(3):
-            gather(p, 1).wait_recv()
-            gather(p, 2).start()
+            gather(p, 0, 0).wait_recv()
+            gather(p, 1, 1).start()
+            gather(p, 1, 2).start()
+        for p in range(3):
+            gather(p, 0, 1).wait_recv()
+            gather(p, 2, 2).start()
         forward(TOK, TOK, 0)
         activate(act, pl.ds(TOK, TOK))
+        for p in range(3):
+            gather(p, 1, 1).wait_recv()
+            gather(p, 3, 2).start()
 
         proj[...] = jnp.zeros_like(proj)
 
@@ -287,27 +303,28 @@
             return 0
 
         lax.fori_loop(0, 4, partial, 0)
-        for p in range(3):
-            gather(p, 2).wait_recv()
-        lax.fori_loop(4, 8, partial, 0)
+        for src in range(4):
+            for p in range(3):
+                gather(p, src, 2).wait_recv()
+            partial(src + 4, 0)
         activate(actf, pl.ds(0, TOK))
 
         def term(r, put):
             grads(actf, slice(0, TOK), mid, lambda p: flip(share_rs(d, p, r)), put)
 
-        reduce_scatter(term, rcvf, rf_s, rf_r)
-        for p in range(3):
-            back[p] = acc[p, 0].astype(BF16)
-            returned(p).start()
-
-        def piece(i, _):
+        def piece(i):
             for kind in (0, 1):
                 forwarded(i, kind).wait_recv()
             forward(2 * TOK + i * CH, CH, i * CH)
-            return 0
-
-        lax.fori_loop(0, NCH, piece, 0)
+
+        reduce_scatter(term, rcvf, rf_s, rf_r, piece)
+        for p in range(3):
+            back[p] = acc[p, 0].astype(BF16)
+        for i in range(2, NCH):
+            piece(i)
         activate(act, pl.ds(2 * TOK, TOK))
+        for p in range(3):
+            returned(p).start()
 
     def own_term(r, put):
         @pl.when(core == 0)
@@ -326,9 +343,8 @@
             returned(p).wait_recv()
             acc[p, 0] = acc[p, 0] + ret[p].astype(F32)
 
-    o_gu[:, 0:FB] = (acc[0, 0] * scale).T
-    o_gu[:, FB:2 * FB] = (acc[1, 0] * scale).T
-    o_dn[...] = acc[2, 0] * scale
+    for p in range(3):
+        out[p] = acc[p, 0]
 
     @pl.when(core == 0)
     def _():
@@ -344,8 +360,8 @@
         for p in range(3):
             weight_slice(p).wait_send()
             returned(p).wait_send()
-            for step in range(3):
-                gather(p, step).wait_send()
+            for src, step in gathers:
+                gather(p, src, step).wait_send()
 
 
 def local(tokens, cotangent, gain, gate_up, down):
@@ -353,14 +369,11 @@
     anywhere = pl.BlockSpec(memory_space=pl.ANY)
     vmem = pl.BlockSpec(memory_space=pltpu.VMEM)
     dma = pltpu.SemaphoreType.DMA
-    return pl.pallas_call(
-        functools.partial(kernel, scale),
-        out_shape=(
-            jax.ShapeDtypeStruct((SL, 2 * FB), F32),
-            jax.ShapeDtypeStruct((FB, SL), F32),
-        ),
+    sums = pl.pallas_call(
+        kernel,
+        out_shape=jax.ShapeDtypeStruct((3, FB, SL), F32),
         in_specs=[anywhere, anywhere, vmem, anywhere, anywhere],
-        out_specs=(vmem, vmem),
+        out_specs=vmem,
         scratch_shapes=[
             pltpu.VMEM((3 * TOK, D), BF16),
             pltpu.VMEM((3 * TOK, D), BF16),
@@ -378,7 +391,7 @@
             pltpu.VMEM((3, FB, SL), BF16),
             pltpu.VMEM((3, FB, SL), BF16),
             dma((4,)),
-            dma((3,)), dma((3,)), dma((3, 3)), dma((3, 3)),
+            dma((3,)), dma((3,)), dma((3, 7)), dma((3, 7)),
             dma((3, 7)), dma((3, 7)), dma((3, 7)), dma((3, 7)),
             dma((NCH, 2)), dma((NCH, 2)), dma((NCH, 2)), dma((NCH, 2)),
             dma((2,)), dma((2,)), dma((3,)), dma((3,)),
@@ -389,6 +402,16 @@
         ),
         name="grads",
     )(tokens, cotangent, gain.reshape(1, D), gate_up, down)
+    return pl.pallas_call(
+        functools.partial(finish, scale),
+        out_shape=(
+            jax.ShapeDtypeStruct((SL, 2 * FB), F32),
+            jax.ShapeDtypeStruct((FB, SL), F32),
+        ),
+        in_specs=[vmem],
+        out_specs=(vmem, vmem),
+        name="scaled",
+    )(sums)
 
 
 def solution(mesh):

time: 117 us -> 108 us (0.923)
  Pallas kernels: 111 us -> 105 us
  local copies, waits for them, and re-layouts: 3.83 us -> 0 us
    pallas_call x1 -> x2, Pallas kernels: 111 us -> 105 us  [the longest x1 103 us: local(): pl.pallas_call(kernel, out_shape=jax.ShapeDtypeStruct((3, FB, SL), F32),...]
    unnamed x2 -> x0, local copies, waits for them, and re-layouts: 3.83 us -> none
where the time goes in v3:
time: 108 us; the launch traced here: 106 us
  Pallas kernels  105 us (97%)
    pallas_call x1, Pallas kernels, local(): pl.pallas_call(kernel, out_shape=jax.ShapeDtypeStruct((3, FB, SL), F32),...  103 us
    pallas_call x1, Pallas kernels, local(): pl.pallas_call(functools.partial(finish, scale), out_shape=(jax.ShapeDtyp...  2.73 us

profile of v3, /device:TPU:24, one launch (start us, length us, event | category | flops | bytes accessed | tf_op | source)
XLA Modules:
  0.0 106.0 jit_solution(9120642386898239608)
XLA Ops:
  0.6 102.6 %grads.1.sums = f32[3,192,512]{2,1,0:T(8,128)} custom-call(bf16[256,4096]{1,0:T(8,128)(2,1)} %tok.1, bf16[256,4096]{1,0:T(8,128)(2,1)} %cot.1, f32[1,4096]{1,0:T(1,128)} %bitcast.1, bf16[4096,384]{1,0:T(8,128)(2,1)} %gu.1, bf16[192,4096]{1,0:T(8,128)(2,1)} %dn.1), custom_call_target="tpu_custom_call" | custom-call | tf_op jit(solution)/shard_map/grads/pallas_call | solution.py:372
  103.2 2.7 %scaled.1 = (f32[512,384]{1,0:T(8,128)}, f32[192,512]{1,0:T(8,128)}) custom-call(f32[3,192,512]{2,1,0:T(8,128)} %grads.1.sums), custom_call_target="tpu_custom_call" | custom-call | tf_op jit(solution)/shard_map/scaled/pallas_call | solution.py:405

commit v4 on v3

--- a/solution.py
+++ b/solution.py
@@ -63,7 +63,7 @@
     out,
     nrm, ctg, wg, wd, wf, wfd, proj, act, actf, snd, rcv, rcvf, acc, back, ret,
     ld_sem, ws_s, ws_r, ag_s, ag_r, rs_s, rs_r, rf_s, rf_r,
-    tk_s, tk_r, fw_s, fw_r, t1_s, t1_r, rt_s, rt_r, go,
+    tk_s, tk_r, in_s, in_r, rt_s, rt_r, go, done,
 ):
     b = lax.axis_index("blk")
     d = lax.axis_index("dp")
@@ -125,14 +125,11 @@
             return remote(cot.at[here], ctg.at[there], tk_s.at[i, 0], tk_r.at[i, 0], prv, df)
         return remote(nrm.at[here], nrm.at[there], tk_s.at[i, 1], tk_r.at[i, 1], prv, df)
 
-    def forwarded(i, kind):
-        there = pl.ds(pl.multiple_of(2 * TOK + i * CH, CH), CH)
-        ref = nrm if kind else ctg
-        return remote(ref.at[there], ref.at[there], fw_s.at[i, kind], fw_r.at[i, kind], other, d)
-
-    mid = pl.ds(TOK, TOK)
-    mid_cot = remote(cot, ctg.at[mid], t1_s.at[0], t1_r.at[0], other, d)
-    mid_nrm = remote(nrm.at[mid], nrm.at[mid], t1_s.at[1], t1_r.at[1], other, d)
+    low, mid = pl.ds(0, TOK), pl.ds(TOK, TOK)
+    low_cot = remote(cot, ctg.at[low], in_s.at[0], in_r.at[0], other, d)
+    low_nrm = remote(nrm.at[low], nrm.at[low], in_s.at[1], in_r.at[1], other, d)
+    mid_cot = remote(cot, ctg.at[mid], in_s.at[2], in_r.at[2], other, d)
+    mid_nrm = remote(nrm.at[mid], nrm.at[mid], in_s.at[3], in_r.at[3], other, d)
 
     def returned(p):
         return remote(back.at[p], ret.at[p], rt_s.at[p], rt_r.at[p], prv, df)
@@ -155,15 +152,16 @@
             ctg[rows, :], wd[...], (((1,), (1,)), ((), ())), preferred_element_type=F32
         )
 
-    def activate(dst, cols):
-        t = proj[...].T
+    def activate(dst, col, n):
+        cols = slice(col, col + n)
+        t = proj[0:n].T
         gate, up, bk = t[0:FB], t[FB:2 * FB], t[2 * FB:3 * FB]
         s = jax.nn.sigmoid(gate)
         dst[0:FB, cols] = (bk * up * (s * (1.0 + gate * (1.0 - s)))).astype(BF16)
         dst[FB:2 * FB, cols] = (bk * gate * s).astype(BF16)
         dst[2 * FB:3 * FB, cols] = (gate * s * up).astype(BF16)
 
-    def reduce_scatter(term, r_ref, s_sem, r_sem, beside_it=None):
+    def reduce_scatter(term, r_ref, s_sem, r_sem, beside_it=lambda k: None):
         def copy(p, slot, step):
             return remote(
                 snd.at[p, slot], r_ref.at[p, slot], s_sem.at[p, slot], r_sem.at[p, slot],
@@ -191,9 +189,8 @@
             return 0
 
         lax.fori_loop(0, 4, first, 0)
+        beside_it(0)
         lax.fori_loop(0, 4, kept, 0)
-        if beside_it is not None:
-            beside_it(0)
         for q in (3, 1, 2, 0):
             for p in range(3):
                 copy(p, q, 0).wait_recv()
@@ -203,18 +200,19 @@
                     copy(p, q + 2, 1).start()
                 else:
                     acc[p, q] = v
-        if beside_it is not None:
-            beside_it(1)
+        beside_it(1)
         for p in range(3):
             copy(p, 5, 1).wait_recv()
             snd[p, 6] = (acc[p, 1] + r_ref[p, 5].astype(F32)).astype(BF16)
             copy(p, 6, 2).start()
+        beside_it(2)
         for p in range(3):
             copy(p, 4, 1).wait_recv()
             acc[p, 0] = acc[p, 0] + r_ref[p, 4].astype(F32)
         for p in range(3):
             copy(p, 6, 2).wait_recv()
             acc[p, 0] = acc[p, 0] + r_ref[p, 6].astype(F32)
+        beside_it(3)
         for p in range(3):
             for slot, step in [(k, 0) for k in range(4)] + [(4, 1), (5, 1), (6, 2)]:
                 copy(p, slot, step).wait_send()
@@ -230,9 +228,11 @@
 
     @pl.when(core == 0)
     def _():
+        low_cot.start()
         load_rest()
         ld_tok.wait()
         normalise(0, TOK)
+        low_nrm.start()
         pl.semaphore_wait(go, 1)
         for i in range(NCH):
             token_piece(i, 0).start()
@@ -241,22 +241,33 @@
         ld_wg.wait()
         ld_wd.wait()
         forward(0, TOK, 0)
-        activate(act, pl.ds(0, TOK))
+        activate(act, 0, TOK)
         mid_cot.wait_recv()
         mid_nrm.wait_recv()
         forward(TOK, TOK, 0)
-        activate(act, pl.ds(TOK, TOK))
+        activate(act, TOK, TOK)
 
         def piece(i, _):
             for kind in (0, 1):
                 token_piece(i, kind).wait_recv()
-                forwarded(i, kind).start()
-
             forward(2 * TOK + i * CH, CH, i * CH)
             return 0
 
         lax.fori_loop(0, NCH, piece, 0)
-        activate(act, pl.ds(2 * TOK, TOK))
+        pl.semaphore_signal(done, inc=1, device_id=(other, d), device_id_type=MESH)
+        activate(act, 2 * TOK, TOK)
+
+        def term(r, put):
+            grads(act, slice(0, 3 * TOK), pl.ds(0, 3 * TOK), lambda p: share_rs(d, p, r), put)
+
+        reduce_scatter(term, rcv, rs_s, rs_r)
+        for p in range(3):
+            out[p] = acc[p, 0]
+        low_cot.wait_send()
+        low_nrm.wait_send()
+        for i in range(NCH):
+            for kind in (0, 1):
+                token_piece(i, kind).wait_send()
 
     @pl.when(core == 1)
     def _():
@@ -267,37 +278,52 @@
         ld_tok.wait()
         normalise(TOK, TOK)
         mid_nrm.start()
-        for p in range(3):
-            weight_slice(p).wait_recv()
-            for step in range(3):
-                gather(p, 0, step).start()
-            if p == 1:
-                pl.semaphore_signal(go, inc=1, device_id=(beside, df), device_id_type=MESH)
         ld_cot.wait()
         ld_wg.wait()
         ld_wd.wait()
-        for p in range(3):
-            gather(p, 0, 0).wait_recv()
-            gather(p, 1, 1).start()
-            gather(p, 1, 2).start()
-        for p in range(3):
-            gather(p, 0, 1).wait_recv()
-            gather(p, 2, 2).start()
         forward(TOK, TOK, 0)
-        activate(act, pl.ds(TOK, TOK))
-        for p in range(3):
-            gather(p, 1, 1).wait_recv()
-            gather(p, 3, 2).start()
+        activate(act, TOK, TOK)
+
+        def term(r, put):
+            grads(act, slice(TOK, 2 * TOK), mid, lambda p: share_rs(d, p, r), put)
+
+        def gathering(k):
+            for p in range(3):
+                if k == 0:
+                    weight_slice(p).wait_recv()
+                    for step in range(3):
+                        gather(p, 0, step).start()
+                    if p == 1:
+                        pl.semaphore_signal(
+                            go, inc=1, device_id=(beside, df), device_id_type=MESH
+                        )
+                elif k == 1:
+                    gather(p, 0, 0).wait_recv()
+                    gather(p, 1, 1).start()
+                    gather(p, 1, 2).start()
+                elif k == 2:
+                    gather(p, 0, 1).wait_recv()
+                    gather(p, 2, 2).start()
+                else:
+                    gather(p, 1, 1).wait_recv()
+                    gather(p, 3, 2).start()
+
+        reduce_scatter(term, rcv, rs_s, rs_r, gathering)
+        for p in range(3):
+            out[p] = acc[p, 0]
 
         proj[...] = jnp.zeros_like(proj)
+        both = pl.ds(0, 2 * TOK)
+        low_cot.wait_recv()
+        low_nrm.wait_recv()
 
         def partial(r, _):
             for p in range(2):
                 j = share_ag(d, p, r)
                 cols = pl.ds(pl.multiple_of(j * SL + p * 256, 256), 256)
-                proj[:, 0:384] += jnp.dot(nrm[mid, cols], wf[p, r], preferred_element_type=F32)
+                proj[:, 0:384] += jnp.dot(nrm[both, cols], wf[p, r], preferred_element_type=F32)
             proj[:, 384:576] += lax.dot_general(
-                ctg[mid, columns(share_ag(d, 2, r), SL)], wfd[r],
+                ctg[both, columns(share_ag(d, 2, r), SL)], wfd[r],
                 (((1,), (1,)), ((), ())), preferred_element_type=F32,
             )
             return 0
@@ -307,54 +333,21 @@
             for p in range(3):
                 gather(p, src, 2).wait_recv()
             partial(src + 4, 0)
-        activate(actf, pl.ds(0, TOK))
-
-        def term(r, put):
-            grads(actf, slice(0, TOK), mid, lambda p: flip(share_rs(d, p, r)), put)
-
-        def piece(i):
-            for kind in (0, 1):
-                forwarded(i, kind).wait_recv()
-            forward(2 * TOK + i * CH, CH, i * CH)
-
-        reduce_scatter(term, rcvf, rf_s, rf_r, piece)
+        activate(actf, 0, 2 * TOK)
+
+        def foreign(r, put):
+            grads(actf, slice(0, 2 * TOK), both, lambda p: flip(share_rs(d, p, r)), put)
+
+        reduce_scatter(foreign, rcvf, rf_s, rf_r)
         for p in range(3):
             back[p] = acc[p, 0].astype(BF16)
-        for i in range(2, NCH):
-            piece(i)
-        activate(act, pl.ds(2 * TOK, TOK))
+        pl.semaphore_wait(done, 1)
         for p in range(3):
             returned(p).start()
-
-    def own_term(r, put):
-        @pl.when(core == 0)
-        def _():
-            grads(act, slice(0, 3 * TOK), pl.ds(0, 3 * TOK), lambda p: share_rs(d, p, r), put)
-
-        @pl.when(core == 1)
-        def _():
-            grads(act, slice(TOK, 3 * TOK), pl.ds(TOK, 2 * TOK), lambda p: share_rs(d, p, r), put)
-
-    reduce_scatter(own_term, rcv, rs_s, rs_r)
-
-    @pl.when(core == 1)
-    def _():
         for p in range(3):
             returned(p).wait_recv()
-            acc[p, 0] = acc[p, 0] + ret[p].astype(F32)
-
-    for p in range(3):
-        out[p] = acc[p, 0]
-
-    @pl.when(core == 0)
-    def _():
-        for i in range(NCH):
-            for kind in (0, 1):
-                token_piece(i, kind).wait_send()
-                forwarded(i, kind).wait_send()
-
-    @pl.when(core == 1)
-    def _():
+            out[p] = out[p] + ret[p].astype(F32)
+
         mid_cot.wait_send()
         mid_nrm.wait_send()
         for p in range(3):
@@ -381,9 +374,9 @@
             pltpu.VMEM((FB, D), BF16),
             pltpu.VMEM((2, 8, 256, 2 * FB), BF16),
             pltpu.VMEM((8, FB, SL), BF16),
-            pltpu.VMEM((TOK, 3 * FB), F32),
+            pltpu.VMEM((2 * TOK, 3 * FB), F32),
             pltpu.VMEM((3 * FB, 3 * TOK), BF16),
-            pltpu.VMEM((3 * FB, TOK), BF16),
+            pltpu.VMEM((3 * FB, 2 * TOK), BF16),
             pltpu.VMEM((3, 7, FB, SL), BF16),
             pltpu.VMEM((3, 7, FB, SL), BF16),
             pltpu.VMEM((3, 7, FB, SL), BF16),
@@ -393,9 +386,8 @@
             dma((4,)),
             dma((3,)), dma((3,)), dma((3, 7)), dma((3, 7)),
             dma((3, 7)), dma((3, 7)), dma((3, 7)), dma((3, 7)),
-            dma((NCH, 2)), dma((NCH, 2)), dma((NCH, 2)), dma((NCH, 2)),
-            dma((2,)), dma((2,)), dma((3,)), dma((3,)),
-            pltpu.SemaphoreType.REGULAR,
+            dma((NCH, 2)), dma((NCH, 2)), dma((4,)), dma((4,)), dma((3,)), dma((3,)),
+            pltpu.SemaphoreType.REGULAR, pltpu.SemaphoreType.REGULAR,
         ],
         compiler_params=pltpu.CompilerParams(
             collective_id=0, has_side_effects=True, vmem_limit_bytes=58 << 20

time: 108 us -> 93.1 us (0.86); the launches traced: 106 us -> 92.4 us
  Pallas kernels: 105 us -> 91.8 us
    pallas_call x1, Pallas kernels: 103 us -> 89 us  [local(): pl.pallas_call(kernel, out_shape=jax.ShapeDtypeStruct((3, FB, SL), F32),...]
where the time goes in v4:
time: 93.1 us; the launch traced here: 92.4 us
  Pallas kernels  91.8 us (99%)
    pallas_call x1, Pallas kernels, local(): pl.pallas_call(kernel, out_shape=jax.ShapeDtypeStruct((3, FB, SL), F32),...  89 us
    pallas_call x1, Pallas kernels, local(): pl.pallas_call(functools.partial(finish, scale), out_shape=(jax.ShapeDtyp...  2.73 us

profile of v4, /device:TPU:24, one launch (start us, length us, event | category | flops | bytes accessed | tf_op | source)
XLA Modules:
  0.0 92.4 jit_solution(15598853366999245946)
XLA Ops:
  0.6 89.0 %grads.1.sums = f32[3,192,512]{2,1,0:T(8,128)} custom-call(bf16[256,4096]{1,0:T(8,128)(2,1)} %tok.1, bf16[256,4096]{1,0:T(8,128)(2,1)} %cot.1, f32[1,4096]{1,0:T(1,128)} %bitcast.1, bf16[4096,384]{1,0:T(8,128)(2,1)} %gu.1, bf16[192,4096]{1,0:T(8,128)(2,1)} %dn.1), custom_call_target="tpu_custom_call" | custom-call | tf_op jit(solution)/shard_map/grads/pallas_call | solution.py:365
  89.7 2.7 %scaled.1 = (f32[512,384]{1,0:T(8,128)}, f32[192,512]{1,0:T(8,128)}) custom-call(f32[3,192,512]{2,1,0:T(8,128)} %grads.1.sums), custom_call_target="tpu_custom_call" | custom-call | tf_op jit(solution)/shard_map/scaled/pallas_call | solution.py:397

commit v5 on v4

--- a/solution.py
+++ b/solution.py
@@ -144,13 +144,19 @@
 
         lax.fori_loop(0, n // 16, body, 0)
 
+    def half_forward(row0, n, to, kind):
+        rows = pl.ds(pl.multiple_of(row0, CH), n)
+        dst = pl.ds(pl.multiple_of(to, CH), n)
+        if kind:
+            proj[dst, 0:384] = jnp.dot(nrm[rows, :], wg[...], preferred_element_type=F32)
+        else:
+            proj[dst, 384:576] = lax.dot_general(
+                ctg[rows, :], wd[...], (((1,), (1,)), ((), ())), preferred_element_type=F32
+            )
+
     def forward(row0, n, to):
-        rows = pl.ds(pl.multiple_of(row0, CH), n)
-        out = pl.ds(pl.multiple_of(to, CH), n)
-        proj[out, 0:384] = jnp.dot(nrm[rows, :], wg[...], preferred_element_type=F32)
-        proj[out, 384:576] = lax.dot_general(
-            ctg[rows, :], wd[...], (((1,), (1,)), ((), ())), preferred_element_type=F32
-        )
+        half_forward(row0, n, to, 0)
+        half_forward(row0, n, to, 1)
 
     def activate(dst, col, n):
         cols = slice(col, col + n)
@@ -250,7 +256,7 @@
         def piece(i, _):
             for kind in (0, 1):
                 token_piece(i, kind).wait_recv()
-            forward(2 * TOK + i * CH, CH, i * CH)
+                half_forward(2 * TOK + i * CH, CH, i * CH, kind)
             return 0
 
         lax.fori_loop(0, NCH, piece, 0)
@@ -364,7 +370,7 @@
     dma = pltpu.SemaphoreType.DMA
     sums = pl.pallas_call(
         kernel,
-        out_shape=jax.ShapeDtypeStruct((3, FB, SL), F32),
+        out_shape=pltpu.VMEM((3, FB, SL), F32),
         in_specs=[anywhere, anywhere, vmem, anywhere, anywhere],
         out_specs=vmem,
         scratch_shapes=[
@@ -403,7 +409,7 @@
         in_specs=[vmem],
         out_specs=(vmem, vmem),
         name="scaled",
-    )(sums)
+    )(pltpu.with_memory_space_constraint(sums, pltpu.VMEM))
 
 
 def solution(mesh):

time: 93.1 us -> 90.8 us (0.975)
  Pallas kernels: 91.8 us -> 89.5 us
    pallas_call x1, Pallas kernels: 2.73 us -> 1.46 us  [local(): pl.pallas_call(functools.partial(finish, scale), out_shape=(jax.ShapeDtyp...]
    pallas_call x1, Pallas kernels: 89 us -> 88 us  [local(): pl.pallas_call(kernel, out_shape=pltpu.VMEM((3, FB, SL), F32), in_specs=[...]
where the time goes in v5:
time: 90.8 us; the launch traced here: 90.1 us
  Pallas kernels  89.5 us (99%)
    pallas_call x1, Pallas kernels, local(): pl.pallas_call(kernel, out_shape=pltpu.VMEM((3, FB, SL), F32), in_specs=[...  88 us

profile of v5, /device:TPU:24, one launch (start us, length us, event | category | flops | bytes accessed | tf_op | source)
XLA Modules:
  0.0 90.1 jit_solution(508327475466078273)
XLA Ops:
  0.6 88.0 %grads.1.sums = f32[3,192,512]{2,1,0:T(8,128)S(1)} custom-call(bf16[256,4096]{1,0:T(8,128)(2,1)} %tok.1, bf16[256,4096]{1,0:T(8,128)(2,1)} %cot.1, f32[1,4096]{1,0:T(1,128)} %bitcast.1, bf16[4096,384]{1,0:T(8,128)(2,1)} %gu.1, bf16[192,4096]{1,0:T(8,128)(2,1)} %dn.1), custom_call_target="tpu_custom_call" | custom-call | tf_op jit(solution)/shard_map/grads/pallas_call | solution.py:371
  88.7 1.5 %scaled.1 = (f32[512,384]{1,0:T(8,128)}, f32[192,512]{1,0:T(8,128)}) custom-call(f32[3,192,512]{2,1,0:T(8,128)S(1)} %grads.1.sums), custom_call_target="tpu_custom_call" | custom-call | tf_op jit(solution)/shard_map/scaled/pallas_call | solution.py:403

commit v6 on v5

--- a/solution.py
+++ b/solution.py
@@ -19,6 +19,7 @@
 CH = 64
 NCH = TOK // CH
 
+HALF = (slice(0, FB // 2), slice(FB // 2, FB))
 ORDERS = (("a", "b", "y"), ("b", "y", "a"), ("y", "a", "b"))
 
 
@@ -174,15 +175,21 @@
                 b, partner(d, ORDERS[p][step]),
             )
 
+        def half(p, slot, step, h):
+            k = 4 + 2 * (slot - 4) + h
+            return remote(
+                snd.at[p, slot, HALF[h]], r_ref.at[p, slot, HALF[h]],
+                s_sem.at[p, k], r_sem.at[p, k], b, partner(d, ORDERS[p][step]),
+            )
+
         def first(i, _):
             q = 3 - 2 * lax.rem(i, 2) - i // 2
 
             def put(p, v):
                 snd[p, q] = v.astype(BF16)
+                copy(p, q, 0).start()
 
             term(q + 4, put)
-            for p in range(3):
-                copy(p, q, 0).start()
             return 0
 
         def kept(i, _):
@@ -195,33 +202,39 @@
             return 0
 
         lax.fori_loop(0, 4, first, 0)
-        beside_it(0)
         lax.fori_loop(0, 4, kept, 0)
         for q in (3, 1, 2, 0):
             for p in range(3):
                 copy(p, q, 0).wait_recv()
-                v = acc[p, q] + r_ref[p, q].astype(F32)
-                if q >= 2:
-                    snd[p, q + 2] = v.astype(BF16)
-                    copy(p, q + 2, 1).start()
-                else:
-                    acc[p, q] = v
+                for h in range(2):
+                    rows = HALF[h]
+                    v = acc[p, q, rows] + r_ref[p, q, rows].astype(F32)
+                    if q >= 2:
+                        snd[p, q + 2, rows] = v.astype(BF16)
+                        half(p, q + 2, 1, h).start()
+                    else:
+                        acc[p, q, rows] = v
         beside_it(1)
-        for p in range(3):
-            copy(p, 5, 1).wait_recv()
-            snd[p, 6] = (acc[p, 1] + r_ref[p, 5].astype(F32)).astype(BF16)
-            copy(p, 6, 2).start()
+        for h in range(2):
+            rows = HALF[h]
+            for p in range(3):
+                half(p, 5, 1, h).wait_recv()
+                snd[p, 6, rows] = (acc[p, 1, rows] + r_ref[p, 5, rows].astype(F32)).astype(BF16)
+                half(p, 6, 2, h).start()
         beside_it(2)
-        for p in range(3):
-            copy(p, 4, 1).wait_recv()
-            acc[p, 0] = acc[p, 0] + r_ref[p, 4].astype(F32)
-        for p in range(3):
-            copy(p, 6, 2).wait_recv()
-            acc[p, 0] = acc[p, 0] + r_ref[p, 6].astype(F32)
+        for slot, step in ((4, 1), (6, 2)):
+            for h in range(2):
+                rows = HALF[h]
+                for p in range(3):
+                    half(p, slot, step, h).wait_recv()
+                    acc[p, 0, rows] = acc[p, 0, rows] + r_ref[p, slot, rows].astype(F32)
         beside_it(3)
         for p in range(3):
-            for slot, step in [(k, 0) for k in range(4)] + [(4, 1), (5, 1), (6, 2)]:
-                copy(p, slot, step).wait_send()
+            for slot in range(4):
+                copy(p, slot, 0).wait_send()
+            for slot, step in ((4, 1), (5, 1), (6, 2)):
+                for h in range(2):
+                    half(p, slot, step, h).wait_send()
 
     def grads(a_ref, a_cols, tok_rows, share, put):
         for p in range(3):
@@ -314,6 +327,7 @@
                     gather(p, 1, 1).wait_recv()
                     gather(p, 3, 2).start()
 
+        gathering(0)
         reduce_scatter(term, rcv, rs_s, rs_r, gathering)
         for p in range(3):
             out[p] = acc[p, 0]
@@ -391,7 +405,7 @@
             pltpu.VMEM((3, FB, SL), BF16),
             dma((4,)),
             dma((3,)), dma((3,)), dma((3, 7)), dma((3, 7)),
-            dma((3, 7)), dma((3, 7)), dma((3, 7)), dma((3, 7)),
+            dma((3, 10)), dma((3, 10)), dma((3, 10)), dma((3, 10)),
             dma((NCH, 2)), dma((NCH, 2)), dma((4,)), dma((4,)), dma((3,)), dma((3,)),
             pltpu.SemaphoreType.REGULAR, pltpu.SemaphoreType.REGULAR,
         ],

time: 90.8 us -> 90.6 us (level)
  no operation moved by 1% of the time
where the time goes in v6:
time: 90.6 us; the launch traced here: 90.4 us
  Pallas kernels  89.8 us (99%)
    pallas_call x1, Pallas kernels, local(): pl.pallas_call(kernel, out_shape=pltpu.VMEM((3, FB, SL), F32), in_specs=[...  88.3 us

profile of v6, /device:TPU:24, one launch (start us, length us, event | category | flops | bytes accessed | tf_op | source)
XLA Modules:
  0.0 90.4 jit_solution(7286206849037645792)
XLA Ops:
  0.6 88.3 %grads.1.sums = f32[3,192,512]{2,1,0:T(8,128)S(1)} custom-call(bf16[256,4096]{1,0:T(8,128)(2,1)} %tok.1, bf16[256,4096]{1,0:T(8,128)(2,1)} %cot.1, f32[1,4096]{1,0:T(1,128)} %bitcast.1, bf16[4096,384]{1,0:T(8,128)(2,1)} %gu.1, bf16[192,4096]{1,0:T(8,128)(2,1)} %dn.1), custom_call_target="tpu_custom_call" | custom-call | tf_op jit(solution)/shard_map/grads/pallas_call | solution.py:385
  88.9 1.5 %scaled.1 = (f32[512,384]{1,0:T(8,128)}, f32[192,512]{1,0:T(8,128)}) custom-call(f32[3,192,512]{2,1,0:T(8,128)S(1)} %grads.1.sums), custom_call_target="tpu_custom_call" | custom-call | tf_op jit(solution)/shard_map/scaled/pallas_call | solution.py:417

commit v7 on v6

--- a/solution.py
+++ b/solution.py
@@ -62,7 +62,7 @@
 def kernel(
     tok, cot, gain, gu, dn,
     out,
-    nrm, ctg, wg, wd, wf, wfd, proj, act, actf, snd, rcv, rcvf, acc, back, ret,
+    nrm, ctg, wg, wd, wf, wfd, proj, act, actf, snd, rcv, rcvf, acc, early, back, ret,
     ld_sem, ws_s, ws_r, ag_s, ag_r, rs_s, rs_r, rf_s, rf_r,
     tk_s, tk_r, in_s, in_r, rt_s, rt_r, go, done,
 ):
@@ -266,6 +266,15 @@
         forward(TOK, TOK, 0)
         activate(act, TOK, TOK)
 
+        def here(r, _):
+            def put(p, v):
+                early[p, r] = v
+
+            grads(act, slice(0, 2 * TOK), pl.ds(0, 2 * TOK), lambda p: share_rs(d, p, r), put)
+            return 0
+
+        lax.fori_loop(0, 8, here, 0)
+
         def piece(i, _):
             for kind in (0, 1):
                 token_piece(i, kind).wait_recv()
@@ -277,7 +286,11 @@
         activate(act, 2 * TOK, TOK)
 
         def term(r, put):
-            grads(act, slice(0, 3 * TOK), pl.ds(0, 3 * TOK), lambda p: share_rs(d, p, r), put)
+            def add(p, v):
+                put(p, early[p, r] + v)
+
+            last = pl.ds(2 * TOK, TOK)
+            grads(act, slice(2 * TOK, 3 * TOK), last, lambda p: share_rs(d, p, r), add)
 
         reduce_scatter(term, rcv, rs_s, rs_r)
         for p in range(3):
@@ -401,6 +414,7 @@
             pltpu.VMEM((3, 7, FB, SL), BF16),
             pltpu.VMEM((3, 7, FB, SL), BF16),
             pltpu.VMEM((3, 4, FB, SL), F32),
+            pltpu.VMEM((3, 8, FB, SL), F32),
             pltpu.VMEM((3, FB, SL), BF16),
             pltpu.VMEM((3, FB, SL), BF16),
             dma((4,)),

time: 90.6 us -> 90.3 us (level)
  no operation moved by 1% of the time
where the time goes in v7:
time: 90.3 us; the launch traced here: 90.2 us
  Pallas kernels  89.5 us (99%)
    pallas_call x1, Pallas kernels, local(): pl.pallas_call(kernel, out_shape=pltpu.VMEM((3, FB, SL), F32), in_specs=[...  88.1 us

profile of v7, /device:TPU:24, one launch (start us, length us, event | category | flops | bytes accessed | tf_op | source)
XLA Modules:
  0.0 90.2 jit_solution(3989283588885560517)
XLA Ops:
  0.6 88.1 %grads.1.sums = f32[3,192,512]{2,1,0:T(8,128)S(1)} custom-call(bf16[256,4096]{1,0:T(8,128)(2,1)} %tok.1, bf16[256,4096]{1,0:T(8,128)(2,1)} %cot.1, f32[1,4096]{1,0:T(1,128)} %bitcast.1, bf16[4096,384]{1,0:T(8,128)(2,1)} %gu.1, bf16[192,4096]{1,0:T(8,128)(2,1)} %dn.1), custom_call_target="tpu_custom_call" | custom-call | tf_op jit(solution)/shard_map/grads/pallas_call | solution.py:398
  88.7 1.5 %scaled.1 = (f32[512,384]{1,0:T(8,128)}, f32[192,512]{1,0:T(8,128)}) custom-call(f32[3,192,512]{2,1,0:T(8,128)S(1)} %grads.1.sums), custom_call_target="tpu_custom_call" | custom-call | tf_op jit(solution)/shard_map/scaled/pallas_call | solution.py:431
